TPU v7x, 32 devices: a whole 2x2x4 slice. The times are simulated.
32 devices in a mesh: tm: 4 (over z), sta: 8 (over y, x, core).
Axes of the slice: x: 2, y: 2, z: 4, core: 2. Of those that a mesh axis runs over, the one named last changes fastest.
Arguments:
- record: bfloat16 [128, 2048], P('sta', 'tm')
- tail: bfloat16 [128, 454], P('sta')
- templates: bfloat16 [128, 200, 512], P('sta'), may hold values from -6 to 6
- live: int32 [128], P('sta'), may hold values 0 or 1
- det_template: int32 [56], P('tm'), may hold values from 0 to 511
- det_start: int32 [56], P('tm'), may hold values from 0 to 2047, as said below
- det_owner: int32 [56], P('tm'), may hold values from 0 to 7, as said below
- det_mask: int32 [56, 128], P('tm', 'sta'), may hold values 0 or 1
Outputs:
- stack: float32 [512, 2048], P('sta', 'tm')
- xcorr: bfloat16 [128, 128, 256], P(('tm', 'sta'))
Inputs may be any that keep to these rules, and one draw needn't show every extreme that they name: `det_start`: the detections of rows b * 14 to (b + 1) * 14 - 1 have their cutouts starting within time block b, samples b * 512 to (b + 1) * 512 - 1. `det_owner`: within the 14 rows of one time block no owner appears more than 4 times, and some owner appears exactly 4 times.
All inputs are finite; a program needn't handle non-finite values. No bound on the sum of `live` or of `det_mask` on one device may be relied on, other than what follows from the above.
Results may differ from a plain program's by a relative error of at most 0.0057.
Values may be sent and summed in bfloat16 or wider, within the bound.
A program may use at most 128 MiB of HBM per device.

v0:
```python
import jax
import jax.numpy as jnp
from jax import lax
from jax.sharding import PartitionSpec as P

CAP = 4


EPSILON = 1e-06


def shifted(value, axis, steps):
    count = lax.axis_size(axis)
    leading, last = (max(0, -steps), min(count, count - steps))
    return lax.ppermute(value, axis, [(source, source + steps) for source in range(leading, last)])


def normalize(templates):
    values = templates.astype(jnp.float32)
    centred = values - jnp.mean(values, axis=1, keepdims=True)
    spread = jnp.mean(centred * centred, axis=1, keepdims=True)
    return (centred / jnp.sqrt(templates.shape[1] * (spread + EPSILON))).astype(jnp.bfloat16)


def local(record, tail, templates, live, det_template, det_start, det_owner, det_mask):
    channel_list, block_len = record.shape
    template_len = templates.shape[1]
    template_count = templates.shape[2]
    border_pad = tail.shape[1]
    lag_count = border_pad - template_len + 2
    windows = block_len + lag_count - 1
    sta_count = lax.axis_size("sta")
    block_index = lax.axis_index("tm")
    following = shifted(record[:, :border_pad], "tm", -1)
    following = jnp.where(block_index == lax.axis_size("tm") - 1, tail, following)
    extended = jnp.concatenate([record, following], axis=1)
    offsets = jnp.arange(template_len)[:, None] + jnp.arange(windows)[None, :]
    unfolded = jnp.take(extended, offsets, axis=1)
    unfolded_wide = unfolded.astype(jnp.float32)
    window_mean = jnp.mean(unfolded_wide, axis=1)
    window_square = jnp.mean(unfolded_wide * unfolded_wide, axis=1)
    weight = live.astype(jnp.float32)[:, None] / jnp.sqrt(
        template_len * (window_square - window_mean * window_mean + EPSILON)
    )
    normed = normalize(templates)
    rescaled_trace = (
        (unfolded[:, :, :block_len].astype(jnp.float32) - window_mean[:, None, :block_len])
        * weight[:, None, :block_len]
    ).astype(jnp.bfloat16)
    own_rows = template_count // sta_count
    total = lax.psum(
        lax.dot_general(
            normed, rescaled_trace, (((0, 1), (0, 1)), ((), ())), preferred_element_type=jnp.float32
        ),
        "sta",
    )
    stack = lax.dynamic_slice_in_dim(total, lax.axis_index("sta") * own_rows, own_rows, 0)
    local_start = det_start - block_index * block_len
    chosen = jnp.take(normed, det_template, axis=2)
    correlated = lax.dot_general(
        chosen, unfolded, (((1,), (1,)), ((0,), (0,))), preferred_element_type=jnp.float32
    )
    correlated = correlated * weight[:, None, :]
    lagged = jax.vmap(
        lambda series, begin: lax.dynamic_slice_in_dim(series, begin, lag_count, 1), in_axes=(1, 0)
    )(correlated, local_start)
    values = (lagged * det_mask.astype(jnp.float32)[:, :, None]).astype(jnp.bfloat16)
    detect_count = det_owner.shape[0]
    positions = jnp.arange(detect_count)
    earlier = (det_owner[None, :] == det_owner[:, None]) & (positions[None, :] < positions[:, None])
    rank = jnp.sum(earlier.astype(jnp.int32), axis=1)
    slot = rank * sta_count + det_owner
    placing = (slot[None, :] == jnp.arange(CAP * sta_count)[:, None]).astype(jnp.bfloat16)
    packed = jnp.dot(
        placing,
        values.reshape(detect_count, channel_list * lag_count),
        preferred_element_type=jnp.float32,
    )
    packed = packed.astype(jnp.bfloat16).reshape(CAP, sta_count, channel_list, lag_count)
    received = lax.all_to_all(packed, "sta", split_axis=1, concat_axis=1, tiled=True)
    xcorr = received.reshape(CAP, sta_count * channel_list, lag_count)
    return (stack, xcorr)


def solution(mesh):
    in_specs = (
        P("sta", "tm"),
        P("sta", None),
        P("sta", None, None),
        P("sta"),
        P("tm"),
        P("tm"),
        P("tm"),
        P("tm", "sta"),
    )
    out_specs = (P("sta", "tm"), P(("tm", "sta"), None, None))
    return jax.shard_map(local, mesh=mesh, in_specs=in_specs, out_specs=out_specs, check_vma=False)
```

profile of v0, /device:TPU:0, one launch (start us, length us, event | category | flops | bytes accessed | tf_op | source)
XLA Modules:
  0.0 470.2 jit_solution(11244376394030251385)
XLA Ops:
  7.2 0.0 all-reduce.3.cloned.1.call-start
  7.2 1.3 collective-permute-start
  8.6 0.7 compare_select_fusion.3
  9.2 0.7 compare_and_fusion
  9.9 0.5 reshape.105
  10.4 0.1 pad_clamp_fusion
  10.5 7.7 %copy.53 = bf16[16,200,512]{1,0,2:T(8,128)(2,1)} copy(bf16[16,200,512]{2,1,0:T(8,128)(2,1)} %param.10) | data formatting | bytes 6553600 | tf_op args[2]
  18.2 0.0 copy-start
  18.2 3.5 convert_reduce_fusion.1
  21.7 0.0 copy-done
  21.7 14.1 %fusion.3 = f32[16,512]{0,1:T(8,128)S(1)} fusion(bf16[16,200,512]{1,0,2:T(8,128)(2,1)S(1)} %copy-done, f32[16,512]{0,1:T(8,128)S(1)} %broadcast_multiply_fusion), kind=kLoop, calls=%fused_computation.10 | loop fusion | flops 6545408 | bytes 3342336 | tf_op jit(solution)/shard_map/reduce_sum | solution.py:21
  35.9 0.0 copy-start.6
  35.9 0.1 multiply_sqrt_fusion
  36.0 0.0 copy-start.7
  36.0 0.0 copy-start.8
  36.0 0.0 copy-start.5
  36.0 0.0 copy-start.3
  36.0 0.0 copy-start.4
  36.0 4.7 %fusion.4 = bf16[16,200,512]{1,0,2:T(8,128)(2,1)} fusion(bf16[16,200,512]{1,0,2:T(8,128)(2,1)S(1)} %copy-done, f32[16,512]{0,1:T(8,128)S(1)} %multiply_sqrt_fusion, f32[16,512]{0,1:T(8,128)S(1)} %broadcast_multiply_fusion), kind=kLoop, calls=%fused_computation.11 | loop fusion | flops 6553600 | bytes 6619136 | tf_op jit(solution)/shard_map/convert_element_type | solution.py:22
  40.8 0.0 copy-done.6
  40.8 0.2 convert_reduce_fusion.2
  40.9 2.7 gather_fusion.1
  43.7 0.1 select_bitcast_fusion.1
  43.8 0.0 copy-done.7
  43.9 0.0 copy-done.8
  43.9 0.0 copy-done.5
  43.9 0.0 collective-permute-done
  43.9 0.0 copy-done.3
  44.0 0.0 copy-done.4
  44.0 0.2 copy.54
  44.2 305.0 %gather_fusion = bf16[153400,16]{1,0:T(8,128)(2,1)} fusion(bf16[16,966]{0,1:T(8,128)(2,1)S(1)} %copy.54, s32[153600]{0:T(1024)S(1)} %pad_clamp_fusion), kind=kCustom, calls=%fused_computation | custom fusion | bytes 10431200 | tf_op jit(solution)/shard_map/jit(_take)/gather | solution.py:38
  349.2 28.8 %copy.55 = bf16[153400,16]{0,1:T(8,128)(2,1)} copy(bf16[153400,16]{1,0:T(8,128)(2,1)} %gather_fusion) | data formatting | bytes 9817600 | tf_op jit(solution)/shard_map/jit(_take)/gather | solution.py:38
  378.0 12.1 %reshape.108 = bf16[200,767,16]{1,0,2:T(8,128)(2,1)} reshape(bf16[153400,16]{0,1:T(8,128)(2,1)} %copy.55) | data formatting | bytes 9817600 | tf_op jit(solution)/shard_map/jit(_take)/gather | solution.py:38
  390.1 0.0 copy-start.2
  390.1 4.6 convert_reduce_fusion
  394.7 0.0 copy-start.1
  394.7 0.1 broadcast_multiply_fusion.1
  394.8 2.1 copy-done.1
  397.0 0.0 copy-done.2
  397.0 4.3 fusion.10
  401.2 0.0 all-reduce.3.cloned.1.call-update
  401.2 3.2 fusion.13
  404.4 5.0 %copy.58 = f32[14,16,767]{1,0,2:T(8,128)} copy(f32[14,16,767]{2,0,1:T(8,128)S(1)} %fusion.13) | data formatting | bytes 1374464 | tf_op jit(solution)/shard_map/mul | solution.py:63
  409.5 4.0 gather_fusion.2
  413.5 0.9 copy.59
  414.4 0.1 multiply_convert_fusion.4
  414.6 0.2 convolution_convert_fusion
  414.8 0.8 copy.60
  415.5 5.1 %all-to-all-start = ((bf16[4,8,16,256]{3,2,0,1:T(8,128)(2,1)}), bf16[4,8,16,256]{3,2,0,1:T(8,128)(2,1)S(1)}, u32[]{:S(2)}, u32[]{:S(2)}) async-start(bf16[4,8,16,256]{3,2,0,1:T(8,128)(2,1)} %copy.60), calls=%async_computation | async-start | bytes 524288 | tf_op jit(solution)/shard_map/all_to_all | solution.py:80
  420.7 6.9 %all-to-all-done = bf16[4,8,16,256]{3,2,0,1:T(8,128)(2,1)S(1)} async-done(((bf16[4,8,16,256]{3,2,0,1:T(8,128)(2,1)}), bf16[4,8,16,256]{3,2,0,1:T(8,128)(2,1)S(1)}, u32[]{:S(2)}, u32[]{:S(2)}) %all-to-all-start) | async-done | bytes 262176 | tf_op jit(solution)/shard_map/all_to_all | solution.py:80
  427.6 0.7 copy.61
  428.3 33.5 %all-reduce.3.cloned.1.call-done = f32[512,512]{1,0:T(8,128)} async-done(((f32[512,512]{1,0:T(8,128)}), f32[512,512]{1,0:T(8,128)}) %all-reduce.3.cloned.1.call-update) | async-done | bytes 1048592 | tf_op jit(solution)/shard_map/psum | solution.py:51
  461.8 1.6 constant_dynamic-slice_fusion
  (14 shorter events, 0.2 us)
Async XLA Ops:
  7.2 454.6 %all-reduce.3.cloned.1.call-start = ((), (), s32[]{:S(2)}) async-start(), calls=%async_computation.1 | async-start | bytes 2097152 | tf_op jit(solution)/shard_map/psum | solution.py:51
  7.2 36.7 %collective-permute-start = (bf16[16,454]{1,0:T(8,128)(2,1)}, bf16[16,454]{1,0:T(8,128)(2,1)S(1)}, u32[]{:S(2)}, u32[]{:S(2)}) collective-permute-start(bf16[16,454]{1,0:T(8,128)(2,1)} %bitcast.33), channel_id=1, source_target_pairs={{8,0},{16,8},{24,16},{9,1},{17,9},{25,17},{10,2},{18,10},{26,18},{... | collective-permute-start | bytes 43592 | tf_op jit(solution)/shard_map/ppermute | solution.py:15
  18.2 3.5 copy-start
  35.9 4.9 %copy-start.6 = (s32[14]{0:T(128)S(1)}, s32[14]{0:T(128)}, u32[]{:S(2)}) copy-start(s32[14]{0:T(128)} %param.14) | copy-start | bytes 172
  36.0 7.8 %copy-start.7 = (s32[14]{0:T(128)S(1)}, s32[14]{0:T(128)}, u32[]{:S(2)}) copy-start(s32[14]{0:T(128)} %param.13) | copy-start | bytes 172
  36.0 7.9 %copy-start.8 = (s32[16]{0:T(128)S(1)}, s32[16]{0:T(128)}, u32[]{:S(2)}) copy-start(s32[16]{0:T(128)} %param.11) | copy-start | bytes 196
  36.0 7.9 %copy-start.5 = (s32[14,16]{1,0:T(8,128)S(1)}, s32[14,16]{1,0:T(8,128)}, u32[]{:S(2)}) copy-start(s32[14,16]{1,0:T(8,128)} %param.15) | copy-start | bytes 2692
  36.0 7.9 %copy-start.3 = (bf16[16,454]{1,0:T(8,128)(2,1)S(1)}, bf16[16,454]{1,0:T(8,128)(2,1)}, u32[]{:S(2)}) copy-start(bf16[16,454]{1,0:T(8,128)(2,1)} %param.9) | copy-start | bytes 43588
  36.0 7.9 %copy-start.4 = (bf16[16,512]{1,0:T(8,128)(2,1)S(1)}, bf16[16,512]{1,0:T(8,128)(2,1)}, u32[]{:S(2)}) copy-start(bf16[16,512]{1,0:T(8,128)(2,1)} %param.8) | copy-start | bytes 49156
  390.1 6.9 %copy-start.2 = (bf16[16,200,512]{1,0,2:T(8,128)(2,1)S(1)}, bf16[16,200,512]{1,0,2:T(8,128)(2,1)}, u32[]{:S(2)}) copy-start(bf16[16,200,512]{1,0,2:T(8,128)(2,1)} %fusion.4) | copy-start | bytes 9830404
  394.7 2.2 copy-start.1
  415.5 12.1 %all-to-all-start = ((bf16[4,8,16,256]{3,2,0,1:T(8,128)(2,1)}), bf16[4,8,16,256]{3,2,0,1:T(8,128)(2,1)S(1)}, u32[]{:S(2)}, u32[]{:S(2)}) async-start(bf16[4,8,16,256]{3,2,0,1:T(8,128)(2,1)} %copy.60), calls=%async_computation | async-start | bytes 524288 | tf_op jit(solution)/shard_map/all_to_all | solution.py:80
Sparse Core Ops, SparseCore 0:
  401.4 60.3 all-reduce.2
where the time goes:
time: 471 us; the launch traced here: 470 us
  local copies, waits for them, and re-layouts  372 us (79%)
  waiting for transfers between devices  40.4 us (9%)
  other arithmetic  29.1 us (6%)
  between operations  14.3 us (3%)
  matrix products  7.64 us (2%)
  starting transfers between devices  6.45 us (1%)
    gather x3, local copies, waits for them, and re-layouts, local(): unfolded = jnp.take(extended, offsets, axis=1)  346 us
    psum x1, waiting for transfers between devices, local(): lax.psum(lax.dot_general(normed, rescaled_trace, (((0, 1), (0, 1)), ((),...  33.5 us
    reduce_sum x1, other arithmetic, normalize(): spread = jnp.mean(centred * centred, axis=1, keepdims=True)  14.1 us
    unnamed x21, local copies, waits for them, and re-layouts  9.96 us
  transfers between devices with their start and end apart: 3, of which 2 were waited for; matrix products, arithmetic and copies ran while one was open for 11% of the time, Pallas kernels for 0%

commit v1 on v0

v1 whole, which is shorter than its diff:
```python
import functools
import jax
import jax.numpy as jnp
from jax import lax
from jax.experimental import pallas as pl
from jax.experimental.pallas import tpu as pltpu
from jax.sharding import PartitionSpec as P

CAP = 4
EPSILON = 1e-06
GROUP = 4
MESH = pl.DeviceIdType.MESH


def round_up(value, unit):
    return (value + unit - 1) // unit * unit


def compute_kernel(template_len, block_len, lag_count, sta_count,
                   live_ref, kind_ref, start_ref, owner_ref,
                   record_ref, following_ref, mask_ref, templates_ref,
                   part_ref, packed_ref,
                   ext, shifts, mean, weight, total, series, onehot, mask, counts):
    channels = record_ref.shape[0]
    detections = kind_ref.shape[0]
    rows = onehot.shape[0]
    kinds = onehot.shape[1]
    width = ext.shape[1]
    windows = mean.shape[1]
    step = pl.program_id(0)
    tm_index = lax.axis_index("tm")

    @pl.when(step == 0)
    def _():
        border = following_ref.shape[1]
        ext[...] = jnp.zeros_like(ext)
        ext[:, :block_len] = record_ref[...].astype(jnp.float32)
        ext[:, block_len:block_len + border] = following_ref[...].astype(jnp.float32)
        sums = ext[...]
        squares = sums * sums

        def left(x, by):
            return pltpu.roll(x, width - by, 1)

        def window_sum(x):
            out, offset, span = None, 0, 1
            powers = []
            while span <= template_len:
                powers.append((span, x))
                if span * 2 <= template_len:
                    x = x + left(x, span)
                span *= 2
            for span, value in reversed(powers):
                if template_len & span:
                    value = value if offset == 0 else left(value, offset)
                    out = value if out is None else out + value
                    offset += span
            return out[:, :windows]

        for r in range(8):
            moved = sums if r == 0 else left(sums, r)
            for j in range(width // 128):
                shifts[j, pl.ds(r, channels, stride=8), :] = moved[:, j * 128:j * 128 + 128]
        average = window_sum(sums) * (1.0 / template_len)
        square = window_sum(squares) * (1.0 / template_len)
        row = lax.broadcasted_iota(jnp.int32, (channels, windows), 0)
        alive = jnp.zeros((channels, windows), jnp.float32)
        for c in range(channels):
            alive = jnp.where(row == c, live_ref[c].astype(jnp.float32), alive)
        mean[...] = average
        weight[...] = alive / jnp.sqrt(template_len * (square - average * average + EPSILON))
        total[...] = jnp.zeros_like(total)
        packed_ref[...] = jnp.zeros_like(packed_ref)
        row = lax.broadcasted_iota(jnp.int32, (rows, kinds), 0)
        column = lax.broadcasted_iota(jnp.int32, (rows, kinds), 1)
        chosen = jnp.full((rows, kinds), -1, jnp.int32)
        for d in range(detections):
            chosen = jnp.where(row == d, kind_ref[d], chosen)
        onehot[...] = (chosen == column).astype(jnp.float32).astype(jnp.bfloat16)
        mask[...] = jnp.zeros_like(mask)
        mask[:detections, :] = mask_ref[...].astype(jnp.float32)

    all_normed, all_scaled = [], []
    for g in range(GROUP):
        c = step * GROUP + g
        values = templates_ref[g].astype(jnp.float32)
        centred = values - jnp.mean(values, axis=0, keepdims=True)
        spread = jnp.mean(centred * centred, axis=0, keepdims=True)
        normed = (centred * lax.rsqrt(template_len * (spread + EPSILON))).astype(jnp.bfloat16)
        trace = jnp.concatenate(
            [shifts[j, pl.ds(pl.multiple_of(c * 8, 8), 8), :] for j in range(width // 128)], axis=1)
        hankel = jnp.concatenate(
            [trace] + [pltpu.roll(trace, width - 8 * s, 1) for s in range(1, 16)], axis=0)
        pieces = []
        for low in range(0, template_len, 128):
            count = min(128, template_len - low)
            pieces.append(hankel[:count, low:low + windows])
        unfolded = jnp.concatenate(pieces, axis=0)
        weights = weight[pl.ds(c, 1), :]
        scaled = ((unfolded[:, :block_len] - mean[pl.ds(c, 1), :block_len])
                  * weights[:, :block_len]).astype(jnp.bfloat16)
        all_normed.append(normed)
        all_scaled.append(scaled)
        picked = lax.dot_general(onehot[...], normed, (((1,), (1,)), ((), ())),
                                 preferred_element_type=jnp.float32).astype(jnp.bfloat16)
        found = jnp.dot(picked, unfolded.astype(jnp.bfloat16), preferred_element_type=jnp.float32)
        lane = lax.broadcasted_iota(jnp.int32, mask.shape, 1)
        used = jnp.sum(jnp.where(lane == c, mask[...], 0.0), axis=1, keepdims=True)
        found = found * weights * used
        for j in range(windows // 128):
            series[j, pl.ds(pl.multiple_of(c * rows, rows), rows), :] = found[:, j * 128:j * 128 + 128]
    total[...] += lax.dot_general(
        jnp.concatenate(all_normed, axis=0), jnp.concatenate(all_scaled, axis=0),
        (((0,), (0,)), ((), ())), preferred_element_type=jnp.float32)

    @pl.when(step == pl.num_programs(0) - 1)
    def _():
        part_ref[...] = total[...].astype(jnp.bfloat16)
        for s in range(sta_count):
            counts[s] = 0
        span = lag_count + 128

        def place(d, carry):
            owner = owner_ref[d]
            rank = counts[owner]
            counts[owner] = rank + 1
            start = start_ref[d] - tm_index * block_len
            base = start // 128
            piece = jnp.concatenate(
                [series[base + j, pl.ds(d, channels, stride=rows), :] for j in range(span // 128)], axis=1)
            moved = pltpu.roll(piece, lax.rem(span - (start - base * 128), span), 1)
            packed_ref[owner * CAP + rank] = moved[:, :lag_count].astype(jnp.bfloat16)
            return carry

        lax.fori_loop(0, detections, place, 0)


def exchange_kernel(sta_count, part_ref, packed_ref, stack_ref, xcorr_ref, landed,
                    send_sem, recv_sem, send_sem2, recv_sem2, own_sem):
    me = lax.axis_index("sta")
    tm = lax.axis_index("tm")
    own_rows = stack_ref.shape[0]
    channels = packed_ref.shape[1]
    barrier = pltpu.get_barrier_semaphore()
    for off in range(1, sta_count):
        pl.semaphore_signal(barrier, inc=1, device_id=(tm, lax.rem(me + off, sta_count)), device_id_type=MESH)
    pl.semaphore_wait(barrier, sta_count - 1)
    mine = xcorr_ref.at[:, pl.ds(pl.multiple_of(me * channels, channels), channels), :]
    copies = []
    for off in range(1, sta_count):
        peer = lax.rem(me + off, sta_count)
        copy = pltpu.make_async_remote_copy(
            src_ref=part_ref.at[pl.ds(pl.multiple_of(peer * own_rows, own_rows), own_rows), :],
            dst_ref=landed.at[off - 1], send_sem=send_sem.at[off - 1], recv_sem=recv_sem.at[off - 1],
            device_id=(tm, peer), device_id_type=MESH)
        copy.start()
        copies.append(copy)
    others = []
    for off in range(1, sta_count):
        peer = lax.rem(me + off, sta_count)
        copy = pltpu.make_async_remote_copy(
            src_ref=packed_ref.at[pl.ds(peer * CAP, CAP)],
            dst_ref=mine, send_sem=send_sem2.at[off - 1], recv_sem=recv_sem2.at[off - 1],
            device_id=(tm, peer), device_id_type=MESH)
        copy.start()
        others.append(copy)
    own = pltpu.make_async_copy(packed_ref.at[pl.ds(me * CAP, CAP)], mine, own_sem)
    own.start()
    summed = part_ref[pl.ds(pl.multiple_of(me * own_rows, own_rows), own_rows), :].astype(jnp.float32)
    for off in range(1, sta_count):
        copies[off - 1].wait()
        summed += landed[off - 1].astype(jnp.float32)
    stack_ref[...] = summed
    own.wait()
    for copy in others:
        copy.wait()


def local(record, tail, templates, live, det_template, det_start, det_owner, det_mask):
    channels, block_len = record.shape
    template_len, template_count = templates.shape[1:]
    border_pad = tail.shape[1]
    lag_count = border_pad - template_len + 2
    sta_count = lax.axis_size("sta")
    tm_count = lax.axis_size("tm")
    detections = det_owner.shape[0]
    rows = round_up(detections, 16)
    windows = block_len + lag_count
    width = round_up(block_len + border_pad + 1, 128)
    following = lax.ppermute(record[:, :border_pad], "tm", [(s, s - 1) for s in range(1, tm_count)])
    following = jnp.where(lax.axis_index("tm") == tm_count - 1, tail, following)
    smem = pl.BlockSpec(memory_space=pltpu.SMEM)
    vmem = pl.BlockSpec(memory_space=pltpu.VMEM)
    part, packed = pl.pallas_call(
        functools.partial(compute_kernel, template_len, block_len, lag_count, sta_count),
        grid=(channels // GROUP,),
        in_specs=[smem] * 4 + [vmem] * 3 + [
            pl.BlockSpec((GROUP, template_len, template_count), lambda i: (i, 0, 0))],
        out_specs=[vmem, vmem],
        out_shape=[
            jax.ShapeDtypeStruct((template_count, block_len), jnp.bfloat16),
            jax.ShapeDtypeStruct((sta_count * CAP, channels, lag_count), jnp.bfloat16)],
        scratch_shapes=[
            pltpu.VMEM((channels, width), jnp.float32),
            pltpu.VMEM((width // 128, channels * 8, 128), jnp.float32),
            pltpu.VMEM((channels, windows), jnp.float32),
            pltpu.VMEM((channels, windows), jnp.float32),
            pltpu.VMEM((template_count, block_len), jnp.float32),
            pltpu.VMEM((windows // 128, channels * rows, 128), jnp.float32),
            pltpu.VMEM((rows, template_count), jnp.bfloat16),
            pltpu.VMEM((rows, channels), jnp.float32),
            pltpu.SMEM((sta_count,), jnp.int32)],
        compiler_params=pltpu.CompilerParams(vmem_limit_bytes=48 * 1024 * 1024),
    )(live, det_template, det_start, det_owner, record, following, det_mask, templates)
    own_rows = template_count // sta_count
    dma = pltpu.SemaphoreType.DMA((sta_count - 1,))
    stack, xcorr = pl.pallas_call(
        functools.partial(exchange_kernel, sta_count),
        in_specs=[vmem, vmem],
        out_specs=[vmem, vmem],
        out_shape=[
            jax.ShapeDtypeStruct((own_rows, block_len), jnp.float32),
            jax.ShapeDtypeStruct((CAP, sta_count * channels, lag_count), jnp.bfloat16)],
        scratch_shapes=[
            pltpu.VMEM((sta_count - 1, own_rows, block_len), jnp.bfloat16),
            dma, dma, dma, dma, pltpu.SemaphoreType.DMA],
        compiler_params=pltpu.CompilerParams(
            collective_id=0, has_side_effects=True, vmem_limit_bytes=48 * 1024 * 1024),
    )(part, packed)
    return stack, xcorr


def solution(mesh):
    in_specs = (
        P("sta", "tm"),
        P("sta", None),
        P("sta", None, None),
        P("sta"),
        P("tm"),
        P("tm"),
        P("tm"),
        P("tm", "sta"),
    )
    out_specs = (P("sta", "tm"), P(("tm", "sta"), None, None))
    return jax.shard_map(local, mesh=mesh, in_specs=in_specs, out_specs=out_specs, check_vma=False)
```

time: 471 us -> 38.7 us (0.08)
  local copies, waits for them, and re-layouts: 372 us -> 7.31 us
  waiting for transfers between devices: 40.4 us -> 5.55 us
  other arithmetic: 29.1 us -> 0.01 us
  Pallas kernels: 0 us -> 23.5 us
  between operations: 14.3 us -> 0.67 us
  matrix products: 7.64 us -> 0 us
  starting transfers between devices: 6.45 us -> 1.29 us
    gather x6 -> x0, local copies, waits for them, and re-layouts: 354 us -> none  [the longest x3 346 us: local(): unfolded = jnp.take(extended, offsets, axis=1)]
    psum x1 -> x0, waiting for transfers between devices: 33.5 us -> none  [local(): lax.psum(lax.dot_general(normed, rescaled_trace, (((0, 1), (0, 1)), ((),...]
    pallas_call x0 -> x2, Pallas kernels: none -> 23.5 us  [the longest x1 12.8 us: local(): pl.pallas_call(functools.partial(exchange_kernel, sta_count), in_specs=[v...]
    reduce_sum x4 -> x0, other arithmetic: 22.5 us -> none  [the longest x1 14.1 us: normalize(): spread = jnp.mean(centred * centred, axis=1, keepdims=True)]
    dot_general x3 -> x0, matrix products: 7.64 us -> none  [the longest x1 4.26 us: local(): lax.dot_general(normed, rescaled_trace, (((0, 1), (0, 1)), ((), ())), pre...]
    all_to_all x1 -> x0, waiting for transfers between devices: 6.94 us -> none  [local(): lax.all_to_all(packed, 'sta', split_axis=1, concat_axis=1, tiled=True)]
    ppermute x1, waiting for transfers between devices: 0.01 us -> 5.55 us  [local(): lax.ppermute(record[:, :border_pad], 'tm', [(s, s - 1) for s in range(1,...]
    all_to_all x1 -> x0, starting transfers between devices: 5.12 us -> none  [local(): lax.all_to_all(packed, 'sta', split_axis=1, concat_axis=1, tiled=True)]
  transfers between devices with their start and end apart: 3 -> 1, of which waited for: 2 -> 1; matrix products, arithmetic and copies ran while one was open for 11% -> 0% of each run, Pallas kernels for 0% -> 0%
where the time goes in v1:
time: 38.7 us; the launch traced here: 38.3 us
  Pallas kernels  23.5 us (61%)
  local copies, waits for them, and re-layouts  7.31 us (19%)
  waiting for transfers between devices  5.55 us (14%)
  starting transfers between devices  1.29 us (3%)
  between operations  0.67 us (2%)
    pallas_call x1, Pallas kernels, local(): pl.pallas_call(functools.partial(exchange_kernel, sta_count), in_specs=[v...  12.8 us
    pallas_call x1, Pallas kernels, local(): pl.pallas_call(functools.partial(compute_kernel, template_len, block_len,...  10.7 us
    unnamed x16, local copies, waits for them, and re-layouts  7.31 us
    ppermute x1, waiting for transfers between devices, local(): lax.ppermute(record[:, :border_pad], 'tm', [(s, s - 1) for s in range(1,...  5.55 us
    ppermute x1, starting transfers between devices, local(): lax.ppermute(record[:, :border_pad], 'tm', [(s, s - 1) for s in range(1,...  1.29 us
  transfers between devices with their start and end apart: 1, of which 1 were waited for; matrix products, arithmetic and copies ran while one was open for 0% of the time, Pallas kernels for 0%

profile of v1, /device:TPU:0, one launch (start us, length us, event | category | flops | bytes accessed | tf_op | source)
XLA Modules:
  0.0 38.3 jit_solution(1268213240634203724)
XLA Ops:
  0.6 1.3 %collective-permute-start = (bf16[16,454]{1,0:T(8,128)(2,1)}, bf16[16,454]{1,0:T(8,128)(2,1)S(1)}, u32[]{:S(2)}, u32[]{:S(2)}) collective-permute-start(bf16[16,454]{1,0:T(8,128)(2,1)} %bitcast.1), channel_id=1, source_target_pairs={{8,0},{16,8},{24,16},{9,1},{17,9},{25,17},{10,2},{18,10},{26,18},{... | collective-permute-start | bytes 43592 | tf_op jit(solution)/shard_map/ppermute | solution.py:190
  1.9 5.5 %collective-permute-done = bf16[16,454]{1,0:T(8,128)(2,1)S(1)} collective-permute-done((bf16[16,454]{1,0:T(8,128)(2,1)}, bf16[16,454]{1,0:T(8,128)(2,1)S(1)}, u32[]{:S(2)}, u32[]{:S(2)}) %collective-permute-start) | collective-permute-done | bytes 14560 | tf_op jit(solution)/shard_map/ppermute | solution.py:190
  7.5 0.0 copy-start
  7.5 1.9 %copy-done = bf16[16,200,512]{2,1,0:T(8,128)(2,1)S(1)} copy-done((bf16[16,200,512]{2,1,0:T(8,128)(2,1)S(1)}, bf16[16,200,512]{2,1,0:T(8,128)(2,1)}, u32[]{:S(2)}) %copy-start) | copy-done | bytes 3276824
  9.4 0.0 copy-start.1
  9.4 0.7 %copy-done.1 = bf16[16,512]{1,0:T(8,128)(2,1)S(1)} copy-done((bf16[16,512]{1,0:T(8,128)(2,1)S(1)}, bf16[16,512]{1,0:T(8,128)(2,1)}, u32[]{:S(2)}) %copy-start.1) | copy-done | bytes 16408
  10.1 0.0 copy-start.2
  10.1 0.7 %copy-done.2 = s32[14,16]{1,0:T(8,128)S(1)} copy-done((s32[14,16]{1,0:T(8,128)S(1)}, s32[14,16]{1,0:T(8,128)}, u32[]{:S(2)}) %copy-start.2) | copy-done | bytes 920
  10.8 0.0 copy-start.3
  10.8 0.7 %copy-done.3 = s32[16]{0:T(128)S(1)} copy-done((s32[16]{0:T(128)S(1)}, s32[16]{0:T(128)}, u32[]{:S(2)}) %copy-start.3) | copy-done | bytes 88
  11.5 0.0 copy-start.4
  11.5 0.7 %copy-done.4 = s32[14]{0:T(128)S(1)} copy-done((s32[14]{0:T(128)S(1)}, s32[14]{0:T(128)}, u32[]{:S(2)}) %copy-start.4) | copy-done | bytes 80
  12.2 0.0 copy-start.5
  12.2 0.7 %copy-done.5 = s32[14]{0:T(128)S(1)} copy-done((s32[14]{0:T(128)S(1)}, s32[14]{0:T(128)}, u32[]{:S(2)}) %copy-start.5) | copy-done | bytes 80
  12.8 0.0 copy-start.6
  12.8 0.7 %copy-done.6 = s32[14]{0:T(128)S(1)} copy-done((s32[14]{0:T(128)S(1)}, s32[14]{0:T(128)}, u32[]{:S(2)}) %copy-start.6) | copy-done | bytes 80
  13.5 10.7 %shard_map.95 = (bf16[512,512]{1,0:T(8,128)(2,1)S(1)}, bf16[32,16,256]{2,1,0:T(8,128)(2,1)S(1)}) custom-call(s32[16]{0:T(128)S(1)} %copy-done.3, s32[14]{0:T(128)S(1)} %copy-done.4, s32[14]{0:T(128)S(1)} %copy-done.5, s32[14]{0:T(128)S(1)} %copy-done.6, bf16[16,512]{1,0:T(8,128)(2,1)S(1)} %copy-done.1, ...), custom_call_target="tpu_custom_call" | custom-call | tf_op jit(solution)/shard_map/pallas_call | solution.py:194
  24.1 12.8 %shard_map.96 = (f32[64,512]{1,0:T(8,128)S(1)}, bf16[4,128,256]{2,1,0:T(8,128)(2,1)S(1)}) custom-call(bf16[512,512]{1,0:T(8,128)(2,1)S(1)} %get-tuple-element.4.part_ref, bf16[32,16,256]{2,1,0:T(8,128)(2,1)S(1)} %get-tuple-element.5.packed_ref), custom_call_target="tpu_custom_call" | custom-call | tf_op jit(solution)/shard_map/pallas_call | solution.py:217
  37.0 0.7 %copy.12 = f32[64,512]{1,0:T(8,128)} copy(f32[64,512]{1,0:T(8,128)S(1)} %get-tuple-element.8) | data formatting | bytes 262144
  37.6 0.7 %copy.13 = bf16[4,128,256]{2,1,0:T(8,128)(2,1)} copy(bf16[4,128,256]{2,1,0:T(8,128)(2,1)S(1)} %get-tuple-element.9) | data formatting | bytes 524288
  (1 shorter events, 0.0 us)
Async XLA Ops:
  0.6 6.9 %collective-permute-start = (bf16[16,454]{1,0:T(8,128)(2,1)}, bf16[16,454]{1,0:T(8,128)(2,1)S(1)}, u32[]{:S(2)}, u32[]{:S(2)}) collective-permute-start(bf16[16,454]{1,0:T(8,128)(2,1)} %bitcast.1), channel_id=1, source_target_pairs={{8,0},{16,8},{24,16},{9,1},{17,9},{25,17},{10,2},{18,10},{26,18},{... | collective-permute-start | bytes 43592 | tf_op jit(solution)/shard_map/ppermute | solution.py:190
  7.5 1.9 %copy-start = (bf16[16,200,512]{2,1,0:T(8,128)(2,1)S(1)}, bf16[16,200,512]{2,1,0:T(8,128)(2,1)}, u32[]{:S(2)}) copy-start(bf16[16,200,512]{2,1,0:T(8,128)(2,1)} %templates_ref.1) | copy-start | bytes 9830404
  9.4 0.7 %copy-start.1 = (bf16[16,512]{1,0:T(8,128)(2,1)S(1)}, bf16[16,512]{1,0:T(8,128)(2,1)}, u32[]{:S(2)}) copy-start(bf16[16,512]{1,0:T(8,128)(2,1)} %record_ref.1) | copy-start | bytes 49156
  10.1 0.7 %copy-start.2 = (s32[14,16]{1,0:T(8,128)S(1)}, s32[14,16]{1,0:T(8,128)}, u32[]{:S(2)}) copy-start(s32[14,16]{1,0:T(8,128)} %mask_ref.1) | copy-start | bytes 2692
  10.8 0.7 %copy-start.3 = (s32[16]{0:T(128)S(1)}, s32[16]{0:T(128)}, u32[]{:S(2)}) copy-start(s32[16]{0:T(128)} %live_ref.1) | copy-start | bytes 196
  11.5 0.7 %copy-start.4 = (s32[14]{0:T(128)S(1)}, s32[14]{0:T(128)}, u32[]{:S(2)}) copy-start(s32[14]{0:T(128)} %kind_ref.1) | copy-start | bytes 172
  12.2 0.7 %copy-start.5 = (s32[14]{0:T(128)S(1)}, s32[14]{0:T(128)}, u32[]{:S(2)}) copy-start(s32[14]{0:T(128)} %start_ref.1) | copy-start | bytes 172
  12.8 0.7 %copy-start.6 = (s32[14]{0:T(128)S(1)}, s32[14]{0:T(128)}, u32[]{:S(2)}) copy-start(s32[14]{0:T(128)} %owner_ref.1) | copy-start | bytes 172

commit v2 on v0

v2 whole, which is shorter than its diff:
```python
import functools
import jax
import jax.numpy as jnp
from jax import lax
from jax.experimental import pallas as pl
from jax.experimental.pallas import tpu as pltpu
from jax.sharding import PartitionSpec as P

CAP = 4
EPSILON = 1e-06
CHUNKS = 4
PAIR = 2
MESH = pl.DeviceIdType.MESH


def round_up(value, unit):
    return (value + unit - 1) // unit * unit


def kernel(lag_count, sta_count, tm_count,
           record_hbm, tail_hbm, templates_hbm, live_hbm, kind_hbm, start_hbm, owner_hbm, mask_hbm,
           stack_ref, xcorr_ref,
           record, tail, templates, live, kinds, starts, owners, used_raw, halo,
           normed, scaled, ext, shifts, mean, weight, series, values, onehot, mask, packed,
           block, kept, sibling_out, sibling_in, pair_out, landed,
           load_sem, template_sem, halo_sem, xs_sem, xr_sem, own_sem, ss_sem, sr_sem, ps_sem, pr_sem):
    channels, block_len = record.shape
    template_len, template_count = templates.shape[1:]
    border = tail.shape[1]
    detections = mask_hbm.shape[0]
    rows = onehot.shape[0]
    width = ext.shape[1]
    windows = mean.shape[1]
    chips = sta_count // 2
    own_rows = stack_ref.shape[0]
    tm = lax.axis_index("tm")
    me = lax.axis_index("sta")
    chip = me // 2
    core = lax.rem(me, 2)
    sibling = me + 1 - 2 * core

    loads = [pltpu.make_async_copy(src, dst, load_sem.at[i]) for i, (src, dst) in enumerate((
        (record_hbm, record), (tail_hbm, tail), (live_hbm, live), (kind_hbm, kinds),
        (start_hbm, starts), (owner_hbm, owners), (mask_hbm, used_raw)))]
    for load in loads:
        load.start()
    per = channels // CHUNKS
    template_loads = [pltpu.make_async_copy(
        templates_hbm.at[pl.ds(i * per, per)], templates.at[pl.ds(i * per, per)], template_sem.at[i])
        for i in range(CHUNKS)]
    for load in template_loads:
        load.start()

    barrier = pltpu.get_barrier_semaphore()
    for off in range(1, sta_count):
        pl.semaphore_signal(barrier, inc=1, device_id=(tm, lax.rem(me + off, sta_count)), device_id_type=MESH)

    @pl.when(tm < tm_count - 1)
    def _():
        pl.semaphore_signal(barrier, inc=1, device_id=(tm + 1, me), device_id_type=MESH)

    pl.semaphore_wait(barrier, sta_count - 1 + (tm > 0).astype(jnp.int32))
    halo_copy = pltpu.make_async_remote_copy(
        src_ref=record_hbm.at[:, pl.ds(0, halo.shape[1])], dst_ref=halo,
        send_sem=halo_sem.at[0], recv_sem=halo_sem.at[1],
        device_id=(tm - 1, me), device_id_type=MESH)

    @pl.when(tm > 0)
    def _():
        halo_copy.start()

    for load in loads:
        load.wait()
    row = lax.broadcasted_iota(jnp.int32, (rows, template_count), 0)
    column = lax.broadcasted_iota(jnp.int32, (rows, template_count), 1)
    chosen = jnp.full((rows, template_count), -1, jnp.int32)
    for d in range(detections):
        chosen = jnp.where(row == d, kinds[d], chosen)
    onehot[...] = (chosen == column).astype(jnp.float32).astype(jnp.bfloat16)
    mask[...] = jnp.zeros_like(mask)
    mask[:detections, :] = used_raw[...].astype(jnp.float32)

    for i in range(CHUNKS):
        template_loads[i].wait()

        def normalize(c, carry):
            wide = templates[c].astype(jnp.float32)
            centred = wide - jnp.mean(wide, axis=0, keepdims=True)
            spread = jnp.mean(centred * centred, axis=0, keepdims=True)
            normed[c] = (centred * lax.rsqrt(template_len * (spread + EPSILON))).astype(jnp.bfloat16)
            return carry

        lax.fori_loop(i * per, (i + 1) * per, normalize, 0)

    last = tm == tm_count - 1

    @pl.when(jnp.logical_not(last))
    def _():
        halo_copy.wait_recv()
        ext[:, block_len:block_len + border] = halo[:, :border].astype(jnp.float32)

    @pl.when(last)
    def _():
        ext[:, block_len:block_len + border] = tail[...].astype(jnp.float32)

    @pl.when(tm > 0)
    def _():
        halo_copy.wait_send()

    ext[:, :block_len] = record[...].astype(jnp.float32)
    lane = lax.broadcasted_iota(jnp.int32, (channels, width), 1)
    sums = jnp.where(lane < block_len + border, ext[...], 0.0)
    squares = sums * sums

    def left(x, by):
        return pltpu.roll(x, width - by, 1)

    def window_sum(x):
        out, offset, span = None, 0, 1
        powers = []
        while span <= template_len:
            powers.append((span, x))
            if span * 2 <= template_len:
                x = x + left(x, span)
            span *= 2
        for span, value in reversed(powers):
            if template_len & span:
                value = value if offset == 0 else left(value, offset)
                out = value if out is None else out + value
                offset += span
        return out[:, :windows]

    for r in range(8):
        moved = sums if r == 0 else left(sums, r)
        for j in range(width // 128):
            shifts[j, pl.ds(r, channels, stride=8), :] = moved[:, j * 128:j * 128 + 128]
    average = window_sum(sums) * (1.0 / template_len)
    square = window_sum(squares) * (1.0 / template_len)
    row = lax.broadcasted_iota(jnp.int32, (channels, windows), 0)
    alive = jnp.zeros((channels, windows), jnp.float32)
    for c in range(channels):
        alive = jnp.where(row == c, live[c].astype(jnp.float32), alive)
    mean[...] = average
    weight[...] = alive / jnp.sqrt(template_len * (square - average * average + EPSILON))

    def unfold(step, carry):
        for g in range(PAIR):
            c = step * PAIR + g
            trace = jnp.concatenate(
                [shifts[j, pl.ds(pl.multiple_of(c * 8, 8), 8), :] for j in range(width // 128)], axis=1)
            hankel = jnp.concatenate(
                [trace] + [pltpu.roll(trace, width - 8 * s, 1) for s in range(1, 16)], axis=0)
            pieces = []
            for low in range(0, template_len, 128):
                count = min(128, template_len - low)
                pieces.append(hankel[:count, low:low + windows])
            unfolded = jnp.concatenate(pieces, axis=0)
            weights = weight[pl.ds(c, 1), :]
            scaled[c] = ((unfolded[:, :block_len] - mean[pl.ds(c, 1), :block_len])
                         * weights[:, :block_len]).astype(jnp.bfloat16)
            picked = lax.dot_general(onehot[...], normed[c], (((1,), (1,)), ((), ())),
                                     preferred_element_type=jnp.float32).astype(jnp.bfloat16)
            found = jnp.dot(picked, unfolded.astype(jnp.bfloat16), preferred_element_type=jnp.float32)
            lane = lax.broadcasted_iota(jnp.int32, mask.shape, 1)
            used = jnp.sum(jnp.where(lane == c, mask[...], 0.0), axis=1, keepdims=True)
            found = found * weights * used
            for j in range(windows // 128):
                series[j, pl.ds(pl.multiple_of(c * rows, rows), rows), :] = found[:, j * 128:j * 128 + 128]
        return carry

    lax.fori_loop(0, channels // PAIR, unfold, 0)

    span = lag_count + 128
    values[...] = jnp.zeros_like(values)

    def cut(d, carry):
        start = jnp.clip(starts[d] - tm * block_len, 0, block_len - 1)
        base = lax.shift_right_logical(start, 7)
        piece = jnp.concatenate(
            [series[base + j, pl.ds(d, channels, stride=rows), :] for j in range(span // 128)], axis=1)
        moved = pltpu.roll(piece, span - (start - base * 128), 1)
        values[pl.ds(pl.multiple_of(d * channels, channels), channels), :] = (
            moved[:, :lag_count].astype(jnp.bfloat16))
        return carry

    lax.fori_loop(0, detections, cut, 0)
    columns = values.shape[0]
    earlier = lax.broadcasted_iota(jnp.int32, (rows, columns), 0)
    spot = lax.broadcasted_iota(jnp.int32, (rows, columns), 1)
    now = spot // channels
    by_row = jnp.full((rows, columns), -1, jnp.int32)
    by_column = jnp.full((rows, columns), -2, jnp.int32)
    for d in range(detections):
        by_row = jnp.where(earlier == d, owners[d], by_row)
        by_column = jnp.where(now == d, owners[d], by_column)
    same = jnp.where((by_row == by_column) & (earlier < now), 1.0, 0.0)
    rank = jnp.sum(same, axis=0, keepdims=True).astype(jnp.int32)
    slot = by_column[:1] * CAP + rank
    place = slot * channels + (spot - now * channels)[:1]
    part = CAP * channels
    for off in list(range(1, sta_count)) + [0]:
        peer = lax.rem(me + off, sta_count)
        target = lax.broadcasted_iota(jnp.int32, (part, columns), 0) + peer * part
        putting = (target == place).astype(jnp.float32).astype(jnp.bfloat16)
        filled = jnp.dot(putting, values[...], preferred_element_type=jnp.float32)
        packed[pl.ds(peer * CAP, CAP)] = filled.astype(jnp.bfloat16).reshape(CAP, channels, lag_count)

    mine = xcorr_ref.at[:, pl.ds(pl.multiple_of(me * channels, channels), channels), :]
    sent = []
    for off in range(1, sta_count):
        peer = lax.rem(me + off, sta_count)
        copy = pltpu.make_async_remote_copy(
            src_ref=packed.at[pl.ds(peer * CAP, CAP)], dst_ref=mine,
            send_sem=xs_sem.at[off - 1], recv_sem=xr_sem.at[off - 1],
            device_id=(tm, peer), device_id_type=MESH)
        copy.start()
        sent.append(copy)
    own = pltpu.make_async_copy(packed.at[pl.ds(me * CAP, CAP)], mine, own_sem)
    own.start()

    count = block.shape[0]
    blocks = template_count // count
    each = count // (2 * own_rows)

    def to_sibling(q):
        return pltpu.make_async_remote_copy(
            src_ref=sibling_out.at[q], dst_ref=sibling_in.at[q],
            send_sem=ss_sem.at[q], recv_sem=sr_sem.at[q],
            device_id=(tm, sibling), device_id_type=MESH)

    def to_chip(off):
        return pltpu.make_async_remote_copy(
            src_ref=pair_out.at[off], dst_ref=landed.at[off],
            send_sem=ps_sem.at[off], recv_sem=pr_sem.at[off],
            device_id=(tm, lax.rem(chip + off, chips) * 2 + core), device_id_type=MESH)

    def pass_on(b):
        for j in range(each):
            q = b * each + j
            to_sibling(q).wait_recv()
            off = lax.rem(q - chip + chips, chips)

            @pl.when(off > 0)
            def _():
                pair_out[off] = (kept[q] + sibling_in[q].astype(jnp.float32)).astype(jnp.bfloat16)
                to_chip(off).start()

    flat = channels * template_len
    for i in range(blocks):
        b = lax.rem(chip // each + 1 + i, blocks)
        block[...] = lax.dot_general(
            normed[:, :, pl.ds(pl.multiple_of(b * count, count), count)].reshape(flat, count),
            scaled[...].reshape(flat, block_len), (((0,), (0,)), ((), ())),
            preferred_element_type=jnp.float32)
        for j in range(each):
            q = b * each + j
            low = (2 * j + core) * own_rows
            other = (2 * j + 1 - core) * own_rows
            sibling_out[q] = block[pl.ds(pl.multiple_of(other, 8), own_rows), :].astype(jnp.bfloat16)
            to_sibling(q).start()
            kept[q] = block[pl.ds(pl.multiple_of(low, 8), own_rows), :]
        if i > 0:
            pass_on(lax.rem(chip // each + i, blocks))
    pass_on(lax.rem(chip // each + blocks, blocks))
    result = kept[chip] + sibling_in[chip].astype(jnp.float32)
    for off in range(1, chips):
        to_chip(off).wait()
        result += landed[off].astype(jnp.float32)
    stack_ref[...] = result
    for q in range(chips):
        to_sibling(q).wait_send()
    own.wait()
    for copy in sent:
        copy.wait()


def local(record, tail, templates, live, det_template, det_start, det_owner, det_mask):
    channels, block_len = record.shape
    template_len, template_count = templates.shape[1:]
    border = tail.shape[1]
    lag_count = border - template_len + 2
    sta_count = lax.axis_size("sta")
    tm_count = lax.axis_size("tm")
    detections = det_owner.shape[0]
    rows = round_up(detections, 16)
    windows = block_len + lag_count
    width = round_up(block_len + border + 1, 128)
    own_rows = template_count // sta_count
    chips = sta_count // 2
    count = max(128, 2 * own_rows)
    bf16, f32, i32 = jnp.bfloat16, jnp.float32, jnp.int32
    dma = pltpu.SemaphoreType.DMA
    anywhere = pl.BlockSpec(memory_space=pl.ANY)
    vmem = pl.BlockSpec(memory_space=pltpu.VMEM)
    return pl.pallas_call(
        functools.partial(kernel, lag_count, sta_count, tm_count),
        in_specs=[anywhere] * 8,
        out_specs=[vmem, vmem],
        out_shape=[
            jax.ShapeDtypeStruct((own_rows, block_len), f32),
            jax.ShapeDtypeStruct((CAP, sta_count * channels, lag_count), bf16)],
        scratch_shapes=[
            pltpu.VMEM(record.shape, bf16),
            pltpu.VMEM(tail.shape, bf16),
            pltpu.VMEM(templates.shape, bf16),
            pltpu.SMEM(live.shape, i32),
            pltpu.SMEM(det_template.shape, i32),
            pltpu.SMEM(det_start.shape, i32),
            pltpu.SMEM(det_owner.shape, i32),
            pltpu.VMEM(det_mask.shape, i32),
            pltpu.VMEM((channels, round_up(border, 128)), bf16),
            pltpu.VMEM(templates.shape, bf16),
            pltpu.VMEM((channels, template_len, block_len), bf16),
            pltpu.VMEM((channels, width), f32),
            pltpu.VMEM((width // 128, channels * 8, 128), f32),
            pltpu.VMEM((channels, windows), f32),
            pltpu.VMEM((channels, windows), f32),
            pltpu.VMEM((windows // 128, channels * rows, 128), f32),
            pltpu.VMEM((rows * channels, lag_count), bf16),
            pltpu.VMEM((rows, template_count), bf16),
            pltpu.VMEM((rows, channels), f32),
            pltpu.VMEM((sta_count * CAP, channels, lag_count), bf16),
            pltpu.VMEM((count, block_len), f32),
            pltpu.VMEM((chips, own_rows, block_len), f32),
            pltpu.VMEM((chips, own_rows, block_len), bf16),
            pltpu.VMEM((chips, own_rows, block_len), bf16),
            pltpu.VMEM((chips, own_rows, block_len), bf16),
            pltpu.VMEM((chips, own_rows, block_len), bf16),
            dma((7,)), dma((CHUNKS,)), dma((2,)),
            dma((sta_count - 1,)), dma((sta_count - 1,)), dma,
            dma((chips,)), dma((chips,)), dma((chips,)), dma((chips,))],
        compiler_params=pltpu.CompilerParams(
            collective_id=0, has_side_effects=True, vmem_limit_bytes=56 * 1024 * 1024),
    )(record, tail, templates, live, det_template, det_start, det_owner, det_mask)


def solution(mesh):
    in_specs = (
        P("sta", "tm"),
        P("sta", None),
        P("sta", None, None),
        P("sta"),
        P("tm"),
        P("tm"),
        P("tm"),
        P("tm", "sta"),
    )
    out_specs = (P("sta", "tm"), P(("tm", "sta"), None, None))
    return jax.shard_map(local, mesh=mesh, in_specs=in_specs, out_specs=out_specs, check_vma=False)
```

time: 471 us -> 26.7 us (0.06)
  local copies, waits for them, and re-layouts: 372 us -> 3.24 us
  waiting for transfers between devices: 40.4 us -> 0 us
  other arithmetic: 29.1 us -> 0 us
  Pallas kernels: 0 us -> 22.6 us
  between operations: 14.3 us -> 0.64 us
  matrix products: 7.64 us -> 0 us
  starting transfers between devices: 6.45 us -> 0 us
    gather x6 -> x0, local copies, waits for them, and re-layouts: 354 us -> none  [the longest x3 346 us: local(): unfolded = jnp.take(extended, offsets, axis=1)]
    psum x1 -> x0, waiting for transfers between devices: 33.5 us -> none  [local(): lax.psum(lax.dot_general(normed, rescaled_trace, (((0, 1), (0, 1)), ((),...]
    pallas_call x0 -> x1, Pallas kernels: none -> 22.6 us  [local(): pl.pallas_call(functools.partial(kernel, lag_count, sta_count, tm_count),...]
    reduce_sum x4 -> x0, other arithmetic: 22.5 us -> none  [the longest x1 14.1 us: normalize(): spread = jnp.mean(centred * centred, axis=1, keepdims=True)]
    dot_general x3 -> x0, matrix products: 7.64 us -> none  [the longest x1 4.26 us: local(): lax.dot_general(normed, rescaled_trace, (((0, 1), (0, 1)), ((), ())), pre...]
    all_to_all x1 -> x0, waiting for transfers between devices: 6.94 us -> none  [local(): lax.all_to_all(packed, 'sta', split_axis=1, concat_axis=1, tiled=True)]
    unnamed x21 -> x2, local copies, waits for them, and re-layouts: 9.96 us -> 3.24 us
    all_to_all x1 -> x0, starting transfers between devices: 5.12 us -> none  [local(): lax.all_to_all(packed, 'sta', split_axis=1, concat_axis=1, tiled=True)]
  transfers between devices with their start and end apart: 3 -> 0, of which waited for: 2 -> 0; matrix products, arithmetic and copies ran while one was open for 11% -> 0% of each run, Pallas kernels for 0% -> 0%
where the time goes in v2:
time: 26.7 us; the launch traced here: 26.5 us
  Pallas kernels  22.6 us (85%)
  local copies, waits for them, and re-layouts  3.24 us (12%)
  between operations  0.64 us (2%)
    pallas_call x1, Pallas kernels, local(): pl.pallas_call(functools.partial(kernel, lag_count, sta_count, tm_count),...  22.6 us
    unnamed x2, local copies, waits for them, and re-layouts  3.24 us

profile of v2, /device:TPU:0, one launch (start us, length us, event | category | flops | bytes accessed | tf_op | source)
XLA Modules:
  0.0 26.5 jit_solution(8407783316717352147)
XLA Ops:
  0.6 22.6 %shard_map.95 = (f32[64,512]{1,0:T(8,128)}, bf16[4,128,256]{2,1,0:T(8,128)(2,1)}) custom-call(bf16[16,512]{1,0:T(8,128)(2,1)} %record_hbm.1, bf16[16,454]{1,0:T(8,128)(2,1)} %tail_hbm.1, bf16[16,200,512]{2,1,0:T(8,128)(2,1)} %templates_hbm.1, s32[16]{0:T(128)} %live_hbm.1, s32[14]{0:T(128)} %kind_hbm.1, s32[14]{0:T(128)} %start_hbm.1, s32[14]{0:T(128)} %owner_hbm.1, ...), custom_call_target="tpu_custom_call" | custom-call | tf_op jit(solution)/shard_map/pallas_call | solution.py:295
  23.3 1.6 %copy.12 = f32[64,512]{1,0:T(8,128)} copy(f32[64,512]{1,0:T(8,128)} %get-tuple-element.4) | data formatting | bytes 262144
  24.8 1.7 %copy.13 = bf16[4,128,256]{2,1,0:T(8,128)(2,1)} copy(bf16[4,128,256]{2,1,0:T(8,128)(2,1)} %get-tuple-element.5) | data formatting | bytes 524288

commit v3 on v2

--- a/solution.py
+++ b/solution.py
@@ -21,7 +21,7 @@
            record_hbm, tail_hbm, templates_hbm, live_hbm, kind_hbm, start_hbm, owner_hbm, mask_hbm,
            stack_ref, xcorr_ref,
            record, tail, templates, live, kinds, starts, owners, used_raw, halo,
-           normed, scaled, ext, shifts, mean, weight, series, values, onehot, mask, packed,
+           normed, scaled, ext, shifts, mean, weight, unfolded, picks, series, values, onehot, mask, packed,
            block, kept, sibling_out, sibling_in, pair_out, landed,
            load_sem, template_sem, halo_sem, xs_sem, xr_sem, own_sem, ss_sem, sr_sem, ps_sem, pr_sem):
     channels, block_len = record.shape
@@ -39,11 +39,6 @@
     core = lax.rem(me, 2)
     sibling = me + 1 - 2 * core
 
-    loads = [pltpu.make_async_copy(src, dst, load_sem.at[i]) for i, (src, dst) in enumerate((
-        (record_hbm, record), (tail_hbm, tail), (live_hbm, live), (kind_hbm, kinds),
-        (start_hbm, starts), (owner_hbm, owners), (mask_hbm, used_raw)))]
-    for load in loads:
-        load.start()
     per = channels // CHUNKS
     template_loads = [pltpu.make_async_copy(
         templates_hbm.at[pl.ds(i * per, per)], templates.at[pl.ds(i * per, per)], template_sem.at[i])
@@ -51,6 +46,11 @@
     for load in template_loads:
         load.start()
 
+    loads = [pltpu.make_async_copy(src, dst, load_sem.at[i]) for i, (src, dst) in enumerate((
+        (record_hbm, record), (tail_hbm, tail), (live_hbm, live), (kind_hbm, kinds),
+        (start_hbm, starts), (owner_hbm, owners), (mask_hbm, used_raw)))]
+    for load in loads:
+        load.start()
     barrier = pltpu.get_barrier_semaphore()
     for off in range(1, sta_count):
         pl.semaphore_signal(barrier, inc=1, device_id=(tm, lax.rem(me + off, sta_count)), device_id_type=MESH)
@@ -59,15 +59,28 @@
     def _():
         pl.semaphore_signal(barrier, inc=1, device_id=(tm + 1, me), device_id_type=MESH)
 
-    pl.semaphore_wait(barrier, sta_count - 1 + (tm > 0).astype(jnp.int32))
-    halo_copy = pltpu.make_async_remote_copy(
-        src_ref=record_hbm.at[:, pl.ds(0, halo.shape[1])], dst_ref=halo,
-        send_sem=halo_sem.at[0], recv_sem=halo_sem.at[1],
-        device_id=(tm - 1, me), device_id_type=MESH)
-
-    @pl.when(tm > 0)
-    def _():
-        halo_copy.start()
+    for i in range(CHUNKS):
+        template_loads[i].wait()
+
+        def normalize(c, carry):
+            wide = templates[c].astype(jnp.float32)
+            centred = wide - jnp.mean(wide, axis=0, keepdims=True)
+            spread = jnp.mean(centred * centred, axis=0, keepdims=True)
+            normed[c] = (centred * lax.rsqrt(template_len * (spread + EPSILON))).astype(jnp.bfloat16)
+            return carry
+
+        lax.fori_loop(i * per, (i + 1) * per, normalize, 0)
+        if i == 0:
+            pl.semaphore_wait(barrier, sta_count - 1 + (tm > 0).astype(jnp.int32))
+            halo_copy = pltpu.make_async_remote_copy(
+                src_ref=record_hbm.at[:, pl.ds(0, halo.shape[1])], dst_ref=halo,
+                send_sem=halo_sem.at[0], recv_sem=halo_sem.at[1],
+                device_id=(tm - 1, me), device_id_type=MESH)
+
+            @pl.when(tm > 0)
+            def _():
+                halo_copy.start()
+
 
     for load in loads:
         load.wait()
@@ -80,18 +93,11 @@
     mask[...] = jnp.zeros_like(mask)
     mask[:detections, :] = used_raw[...].astype(jnp.float32)
 
-    for i in range(CHUNKS):
-        template_loads[i].wait()
-
-        def normalize(c, carry):
-            wide = templates[c].astype(jnp.float32)
-            centred = wide - jnp.mean(wide, axis=0, keepdims=True)
-            spread = jnp.mean(centred * centred, axis=0, keepdims=True)
-            normed[c] = (centred * lax.rsqrt(template_len * (spread + EPSILON))).astype(jnp.bfloat16)
-            return carry
-
-        lax.fori_loop(i * per, (i + 1) * per, normalize, 0)
-
+    flat = channels * template_len
+    picked = lax.dot_general(onehot[...], normed[...].reshape(flat, template_count), (((1,), (1,)), ((), ())),
+                             preferred_element_type=jnp.float32)
+    for c in range(channels):
+        picks[c] = picked[:, c * template_len:(c + 1) * template_len].astype(jnp.bfloat16)
     last = tm == tm_count - 1
 
     @pl.when(jnp.logical_not(last))
@@ -148,75 +154,25 @@
             c = step * PAIR + g
             trace = jnp.concatenate(
                 [shifts[j, pl.ds(pl.multiple_of(c * 8, 8), 8), :] for j in range(width // 128)], axis=1)
-            hankel = jnp.concatenate(
-                [trace] + [pltpu.roll(trace, width - 8 * s, 1) for s in range(1, 16)], axis=0)
-            pieces = []
-            for low in range(0, template_len, 128):
-                count = min(128, template_len - low)
-                pieces.append(hankel[:count, low:low + windows])
-            unfolded = jnp.concatenate(pieces, axis=0)
-            weights = weight[pl.ds(c, 1), :]
-            scaled[c] = ((unfolded[:, :block_len] - mean[pl.ds(c, 1), :block_len])
-                         * weights[:, :block_len]).astype(jnp.bfloat16)
-            picked = lax.dot_general(onehot[...], normed[c], (((1,), (1,)), ((), ())),
-                                     preferred_element_type=jnp.float32).astype(jnp.bfloat16)
-            found = jnp.dot(picked, unfolded.astype(jnp.bfloat16), preferred_element_type=jnp.float32)
-            lane = lax.broadcasted_iota(jnp.int32, mask.shape, 1)
-            used = jnp.sum(jnp.where(lane == c, mask[...], 0.0), axis=1, keepdims=True)
-            found = found * weights * used
-            for j in range(windows // 128):
-                series[j, pl.ds(pl.multiple_of(c * rows, rows), rows), :] = found[:, j * 128:j * 128 + 128]
+            weights = weight[pl.ds(c, 1), :block_len]
+            average = mean[pl.ds(c, 1), :block_len]
+            raw, fine = {}, {}
+            for s in range(0, 16, 2):
+                upper = trace if s == 0 else pltpu.roll(trace, width - 8 * s, 1)
+                both = jnp.concatenate([upper, pltpu.roll(trace, width - 8 * s - 8, 1)], axis=0)
+                for low in range(0, template_len, 128):
+                    first = low + 8 * s
+                    used = min(16, template_len - first)
+                    if used > 0:
+                        piece = both[:used, low:low + windows]
+                        raw[first] = piece.astype(jnp.bfloat16)
+                        fine[first] = ((piece[:, :block_len] - average) * weights).astype(jnp.bfloat16)
+            order = sorted(raw)
+            unfolded[c] = jnp.concatenate([raw[k] for k in order], axis=0)
+            scaled[c] = jnp.concatenate([fine[k] for k in order], axis=0)
         return carry
 
     lax.fori_loop(0, channels // PAIR, unfold, 0)
-
-    span = lag_count + 128
-    values[...] = jnp.zeros_like(values)
-
-    def cut(d, carry):
-        start = jnp.clip(starts[d] - tm * block_len, 0, block_len - 1)
-        base = lax.shift_right_logical(start, 7)
-        piece = jnp.concatenate(
-            [series[base + j, pl.ds(d, channels, stride=rows), :] for j in range(span // 128)], axis=1)
-        moved = pltpu.roll(piece, span - (start - base * 128), 1)
-        values[pl.ds(pl.multiple_of(d * channels, channels), channels), :] = (
-            moved[:, :lag_count].astype(jnp.bfloat16))
-        return carry
-
-    lax.fori_loop(0, detections, cut, 0)
-    columns = values.shape[0]
-    earlier = lax.broadcasted_iota(jnp.int32, (rows, columns), 0)
-    spot = lax.broadcasted_iota(jnp.int32, (rows, columns), 1)
-    now = spot // channels
-    by_row = jnp.full((rows, columns), -1, jnp.int32)
-    by_column = jnp.full((rows, columns), -2, jnp.int32)
-    for d in range(detections):
-        by_row = jnp.where(earlier == d, owners[d], by_row)
-        by_column = jnp.where(now == d, owners[d], by_column)
-    same = jnp.where((by_row == by_column) & (earlier < now), 1.0, 0.0)
-    rank = jnp.sum(same, axis=0, keepdims=True).astype(jnp.int32)
-    slot = by_column[:1] * CAP + rank
-    place = slot * channels + (spot - now * channels)[:1]
-    part = CAP * channels
-    for off in list(range(1, sta_count)) + [0]:
-        peer = lax.rem(me + off, sta_count)
-        target = lax.broadcasted_iota(jnp.int32, (part, columns), 0) + peer * part
-        putting = (target == place).astype(jnp.float32).astype(jnp.bfloat16)
-        filled = jnp.dot(putting, values[...], preferred_element_type=jnp.float32)
-        packed[pl.ds(peer * CAP, CAP)] = filled.astype(jnp.bfloat16).reshape(CAP, channels, lag_count)
-
-    mine = xcorr_ref.at[:, pl.ds(pl.multiple_of(me * channels, channels), channels), :]
-    sent = []
-    for off in range(1, sta_count):
-        peer = lax.rem(me + off, sta_count)
-        copy = pltpu.make_async_remote_copy(
-            src_ref=packed.at[pl.ds(peer * CAP, CAP)], dst_ref=mine,
-            send_sem=xs_sem.at[off - 1], recv_sem=xr_sem.at[off - 1],
-            device_id=(tm, peer), device_id_type=MESH)
-        copy.start()
-        sent.append(copy)
-    own = pltpu.make_async_copy(packed.at[pl.ds(me * CAP, CAP)], mine, own_sem)
-    own.start()
 
     count = block.shape[0]
     blocks = template_count // count
@@ -245,9 +201,87 @@
                 pair_out[off] = (kept[q] + sibling_in[q].astype(jnp.float32)).astype(jnp.bfloat16)
                 to_chip(off).start()
 
-    flat = channels * template_len
+    home = chip // each
+
+    def nth(i):
+        flip, out, bit = blocks - 1 - i, 0, 1
+        while bit < blocks:
+            digit = lax.rem(home // bit, 2)
+            out = out + bit * (1 - digit if flip & bit else digit)
+            bit *= 2
+        return out
+
     for i in range(blocks):
-        b = lax.rem(chip // each + 1 + i, blocks)
+        b = nth(i)
+        if i == blocks - 1:
+            span = lag_count + 128
+            values[...] = jnp.zeros_like(values)
+
+            def find(step, carry):
+                for g in range(4):
+                    c = step * 4 + g
+                    found = jnp.dot(picks[c], unfolded[c], preferred_element_type=jnp.float32)
+                    lane = lax.broadcasted_iota(jnp.int32, mask.shape, 1)
+                    used = jnp.sum(jnp.where(lane == c, mask[...], 0.0), axis=1, keepdims=True)
+                    found = found * weight[pl.ds(c, 1), :] * used
+                    for j in range(windows // 128):
+                        series[j, pl.ds(pl.multiple_of(c * rows, rows), rows), :] = found[:, j * 128:j * 128 + 128]
+                return carry
+
+            lax.fori_loop(0, channels // 4, find, 0)
+            pass_on(nth(i - 1))
+
+            def cut(d):
+                start = jnp.clip(starts[d] - tm * block_len, 0, block_len - 1)
+                base = lax.shift_right_logical(start, 7)
+                piece = jnp.concatenate(
+                    [series[base + j, pl.ds(d, channels, stride=rows), :] for j in range(span // 128)], axis=1)
+                moved = pltpu.roll(piece, span - (start - base * 128), 1)
+                values[pl.ds(pl.multiple_of(d * channels, channels), channels), :] = (
+                    moved[:, :lag_count].astype(jnp.bfloat16))
+
+            run = max(n for n in range(1, 9) if detections % n == 0)
+
+            def cut_some(step, carry):
+                for g in range(run):
+                    cut(step * run + g)
+                return carry
+
+            lax.fori_loop(0, detections // run, cut_some, 0)
+            columns = values.shape[0]
+            earlier = lax.broadcasted_iota(jnp.int32, (rows, columns), 0)
+            spot = lax.broadcasted_iota(jnp.int32, (rows, columns), 1)
+            now = spot // channels
+            by_row = jnp.full((rows, columns), -1, jnp.int32)
+            by_column = jnp.full((rows, columns), -2, jnp.int32)
+            for d in range(detections):
+                by_row = jnp.where(earlier == d, owners[d], by_row)
+                by_column = jnp.where(now == d, owners[d], by_column)
+            same = jnp.where((by_row == by_column) & (earlier < now), 1.0, 0.0)
+            rank = jnp.sum(same, axis=0, keepdims=True).astype(jnp.int32)
+            slot = by_column[:1] * CAP + rank
+            place = slot * channels + (spot - now * channels)[:1]
+            part = CAP * channels
+            for off in list(range(1, sta_count)) + [0]:
+                peer = lax.rem(me + off, sta_count)
+                target = lax.broadcasted_iota(jnp.int32, (part, columns), 0) + peer * part
+                putting = (target == place).astype(jnp.float32).astype(jnp.bfloat16)
+                filled = jnp.dot(putting, values[...], preferred_element_type=jnp.float32)
+                packed[pl.ds(peer * CAP, CAP)] = filled.astype(jnp.bfloat16).reshape(CAP, channels, lag_count)
+
+            mine = xcorr_ref.at[:, pl.ds(pl.multiple_of(me * channels, channels), channels), :]
+            sent = []
+            for off in range(1, sta_count):
+                peer = lax.rem(me + off, sta_count)
+                copy = pltpu.make_async_remote_copy(
+                    src_ref=packed.at[pl.ds(peer * CAP, CAP)], dst_ref=mine,
+                    send_sem=xs_sem.at[off - 1], recv_sem=xr_sem.at[off - 1],
+                    device_id=(tm, peer), device_id_type=MESH)
+                copy.start()
+                sent.append(copy)
+            own = pltpu.make_async_copy(packed.at[pl.ds(me * CAP, CAP)], mine, own_sem)
+            own.start()
+
         block[...] = lax.dot_general(
             normed[:, :, pl.ds(pl.multiple_of(b * count, count), count)].reshape(flat, count),
             scaled[...].reshape(flat, block_len), (((0,), (0,)), ((), ())),
@@ -259,9 +293,9 @@
             sibling_out[q] = block[pl.ds(pl.multiple_of(other, 8), own_rows), :].astype(jnp.bfloat16)
             to_sibling(q).start()
             kept[q] = block[pl.ds(pl.multiple_of(low, 8), own_rows), :]
-        if i > 0:
-            pass_on(lax.rem(chip // each + i, blocks))
-    pass_on(lax.rem(chip // each + blocks, blocks))
+        if 0 < i < blocks - 1:
+            pass_on(nth(i - 1))
+    pass_on(nth(blocks - 1))
     result = kept[chip] + sibling_in[chip].astype(jnp.float32)
     for off in range(1, chips):
         to_chip(off).wait()
@@ -315,6 +349,8 @@
             pltpu.VMEM((width // 128, channels * 8, 128), f32),
             pltpu.VMEM((channels, windows), f32),
             pltpu.VMEM((channels, windows), f32),
+            pltpu.VMEM((channels, template_len, windows), bf16),
+            pltpu.VMEM((channels, rows, template_len), bf16),
             pltpu.VMEM((windows // 128, channels * rows, 128), f32),
             pltpu.VMEM((rows * channels, lag_count), bf16),
             pltpu.VMEM((rows, template_count), bf16),

time: 26.7 us -> 24.7 us (0.925)
  Pallas kernels: 22.6 us -> 20.6 us
    pallas_call x1, Pallas kernels: 22.6 us -> 20.6 us  [local(): pl.pallas_call(functools.partial(kernel, lag_count, sta_count, tm_count),...]
where the time goes in v3:
time: 24.7 us; the launch traced here: 24.4 us
  Pallas kernels  20.6 us (83%)
  local copies, waits for them, and re-layouts  3.24 us (13%)
  between operations  0.64 us (3%)
    pallas_call x1, Pallas kernels, local(): pl.pallas_call(functools.partial(kernel, lag_count, sta_count, tm_count),...  20.6 us
    unnamed x2, local copies, waits for them, and re-layouts  3.24 us

profile of v3, /device:TPU:0, one launch (start us, length us, event | category | flops | bytes accessed | tf_op | source)
XLA Modules:
  0.0 24.4 jit_solution(10852545588501672230)
XLA Ops:
  0.6 20.6 %shard_map.95 = (f32[64,512]{1,0:T(8,128)}, bf16[4,128,256]{2,1,0:T(8,128)(2,1)}) custom-call(bf16[16,512]{1,0:T(8,128)(2,1)} %record_hbm.1, bf16[16,454]{1,0:T(8,128)(2,1)} %tail_hbm.1, bf16[16,200,512]{2,1,0:T(8,128)(2,1)} %templates_hbm.1, s32[16]{0:T(128)} %live_hbm.1, s32[14]{0:T(128)} %kind_hbm.1, s32[14]{0:T(128)} %start_hbm.1, s32[14]{0:T(128)} %owner_hbm.1, ...), custom_call_target="tpu_custom_call" | custom-call | tf_op jit(solution)/shard_map/pallas_call | solution.py:329
  21.2 1.6 %copy.12 = f32[64,512]{1,0:T(8,128)} copy(f32[64,512]{1,0:T(8,128)} %get-tuple-element.4) | data formatting | bytes 262144
  22.8 1.7 %copy.13 = bf16[4,128,256]{2,1,0:T(8,128)(2,1)} copy(bf16[4,128,256]{2,1,0:T(8,128)(2,1)} %get-tuple-element.5) | data formatting | bytes 524288

commit v4 on v3

--- a/solution.py
+++ b/solution.py
@@ -213,7 +213,7 @@
 
     for i in range(blocks):
         b = nth(i)
-        if i == blocks - 1:
+        if i == 1:
             span = lag_count + 128
             values[...] = jnp.zeros_like(values)
 
@@ -293,7 +293,7 @@
             sibling_out[q] = block[pl.ds(pl.multiple_of(other, 8), own_rows), :].astype(jnp.bfloat16)
             to_sibling(q).start()
             kept[q] = block[pl.ds(pl.multiple_of(low, 8), own_rows), :]
-        if 0 < i < blocks - 1:
+        if i > 1:
             pass_on(nth(i - 1))
     pass_on(nth(blocks - 1))
     result = kept[chip] + sibling_in[chip].astype(jnp.float32)

time: 24.7 us -> 25.3 us (1.024)
  Pallas kernels: 20.6 us -> 21.2 us
    pallas_call x1, Pallas kernels: 20.6 us -> 21.2 us  [local(): pl.pallas_call(functools.partial(kernel, lag_count, sta_count, tm_count),...]
where the time goes in v4:
time: 25.3 us; the launch traced here: 25.1 us
  Pallas kernels  21.2 us (84%)
  local copies, waits for them, and re-layouts  3.24 us (13%)
  between operations  0.64 us (3%)
    pallas_call x1, Pallas kernels, local(): pl.pallas_call(functools.partial(kernel, lag_count, sta_count, tm_count),...  21.2 us
    unnamed x2, local copies, waits for them, and re-layouts  3.24 us

profile of v4, /device:TPU:0, one launch (start us, length us, event | category | flops | bytes accessed | tf_op | source)
XLA Modules:
  0.0 25.1 jit_solution(15589080666918295900)
XLA Ops:
  0.6 21.2 %shard_map.95 = (f32[64,512]{1,0:T(8,128)}, bf16[4,128,256]{2,1,0:T(8,128)(2,1)}) custom-call(bf16[16,512]{1,0:T(8,128)(2,1)} %record_hbm.1, bf16[16,454]{1,0:T(8,128)(2,1)} %tail_hbm.1, bf16[16,200,512]{2,1,0:T(8,128)(2,1)} %templates_hbm.1, s32[16]{0:T(128)} %live_hbm.1, s32[14]{0:T(128)} %kind_hbm.1, s32[14]{0:T(128)} %start_hbm.1, s32[14]{0:T(128)} %owner_hbm.1, ...), custom_call_target="tpu_custom_call" | custom-call | tf_op jit(solution)/shard_map/pallas_call | solution.py:329
  21.9 1.6 %copy.12 = f32[64,512]{1,0:T(8,128)} copy(f32[64,512]{1,0:T(8,128)} %get-tuple-element.4) | data formatting | bytes 262144
  23.4 1.7 %copy.13 = bf16[4,128,256]{2,1,0:T(8,128)(2,1)} copy(bf16[4,128,256]{2,1,0:T(8,128)(2,1)} %get-tuple-element.5) | data formatting | bytes 524288
